TPU v7x, 256 devices: a whole 4x4x8 slice. The times are simulated.
256 devices in a mesh: dp: 8 (over z), vocab: 32 (over x, y, core).
Axes of the slice: x: 4, y: 4, z: 8, core: 2. Of those that a mesh axis runs over, the one named last changes fastest.
Arguments:
- hidden: bfloat16 [1024, 8192], P('vocab', 'dp'), as said below
- labels: int32 [1024], P('dp'), may hold values from 0 to 65535
- head_weight: bfloat16 [65536, 8192], P('vocab', 'dp'), as said below
- hess_old: bfloat16 [65536, 8192], P('vocab', 'dp'), may hold values from 2.712477e-08 to 2.7008355e-07
Outputs:
- update: bfloat16 [65536, 8192], P('vocab', 'dp')
Inputs may be any that keep to these rules, and one draw needn't show every extreme that they name: hidden holds entries of order one, at most 8 in magnitude. head_weight holds entries of magnitude about 3 / sqrt(8192).
All inputs are finite; a program needn't handle non-finite values.
Results may differ from a plain program's by a relative error of at most 0.006.
Values may be sent and summed in bfloat16 or wider, within the bound.
A program may use at most 64 MiB of HBM per device.

v0:
```python
import jax
import jax.numpy as jnp
from jax import lax
from jax.sharding import PartitionSpec as P


def softmax_by_tokens(logits):
    peak = lax.pmax(jnp.max(logits, axis=1), "vocab")
    total = lax.psum(jnp.sum(jnp.exp(logits - peak[:, None]), axis=1), "vocab")
    return jnp.exp(logits - peak[:, None]) / total[:, None]


def local(hidden, labels, head_weight, hess_old):
    v_dev = head_weight.shape[0]
    all_hidden = lax.all_gather(hidden, "vocab", axis=0, tiled=True)
    vocab_start = lax.axis_index("vocab") * v_dev
    rows = all_hidden
    logits = lax.psum_scatter(
        lax.dot_general(
            rows, head_weight, (((1,), (1,)), ((), ())), preferred_element_type=jnp.float32
        ),
        "dp",
        scatter_dimension=0,
        tiled=True,
    )
    probs = softmax_by_tokens(logits)
    columns = vocab_start + lax.broadcasted_iota(jnp.int32, (1, v_dev), 1)
    resid = (probs - (labels[:, None] == columns).astype(jnp.float32)).astype(jnp.bfloat16)
    rows = all_hidden
    sums = lax.dot_general(
        lax.all_gather(resid, "dp", axis=0, tiled=True),
        rows,
        (((0,), (0,)), ((), ())),
        preferred_element_type=jnp.float32,
    )
    fresh = 0.9 * hess_old.astype(jnp.float32) + 0.1 * sums * sums
    return jnp.clip(sums / (10000.0 * fresh), -1.0, 1.0).astype(jnp.bfloat16)


def solution(mesh):
    in_specs = (P("vocab", "dp"), P("dp"), P("vocab", "dp"), P("vocab", "dp"))
    out_specs = P("vocab", "dp")
    return jax.shard_map(local, mesh=mesh, in_specs=in_specs, out_specs=out_specs, check_vma=False)
```

profile of v0, /device:TPU:1, one launch (start us, length us, event | category | flops | bytes accessed | tf_op | source)
XLA Modules:
  0.0 368.6 jit_solution(5562532557551324165)
XLA Ops:
  6.5 0.0 all-gather.3.cloned.1.call-start
  6.5 0.7 all-gather.3.cloned.1.call-update
  7.3 0.0 reduce-scatter.2.cloned.1.call-start
  7.3 55.7 %all-gather.3.cloned.1.call-done = bf16[1024,1024]{1,0:T(8,128)(2,1)} async-done(((bf16[32,1024]{1,0:T(8,128)(2,1)}), bf16[1024,1024]{1,0:T(8,128)(2,1)}) %all-gather.3.cloned.1.call-update) | async-done | bytes 2097168 | tf_op jit(solution)/shard_map/all_gather | solution.py:15
  63.0 10.6 %fusion.6 = f32[1024,2048]{1,0:T(8,128)} fusion(bf16[1024,1024]{1,0:T(8,128)(2,1)} %all-gather.3.cloned.1.call-done, bf16[2048,1024]{1,0:T(8,128)(2,1)} %param.6), kind=kOutput, calls=%fused_computation.10 | convolution fusion | flops 4294967296 | bytes 14680064 | tf_op jit(solution)/shard_map/dot_general | solution.py:19
  73.6 0.0 copy-start
  73.6 0.0 reduce-scatter.2.cloned.1.call-update
  73.6 0.0 copy-start.1
  73.6 0.0 all-gather.5.cloned.1.call-start
  73.7 93.9 %reduce-scatter.2.cloned.1.call-done = f32[128,2048]{1,0:T(8,128)} async-done(((f32[1024,2048]{1,0:T(8,128)}), f32[128,2048]{1,0:T(8,128)}) %reduce-scatter.2.cloned.1.call-update) | async-done | bytes 1048592 | tf_op jit(solution)/shard_map/reduce_scatter | solution.py:18
  167.6 1.4 reduce_max.9
  168.9 62.7 %pmax.7 = f32[128]{0:T(128)S(1)} all-reduce(f32[128]{0:T(128)S(1)} %reduce_max.9), channel_id=1, replica_groups=mesh['dp'=8,'vocab'=32] {'vocab'}, use_global_device_ids=true, to_apply=%region_2.0 | all-reduce | flops 128 | bytes 1024 | tf_op jit(solution)/shard_map/pmax | solution.py:8
  231.6 1.5 fusion.5
  233.1 67.0 %psum.7 = f32[128]{0:T(128)S(1)} all-reduce(f32[128]{0:T(128)S(1)} %fusion.5), channel_id=1, replica_groups=mesh['dp'=8,'vocab'=32] {'vocab'}, use_global_device_ids=true, to_apply=%region_4.0 | all-reduce | flops 128 | bytes 1024 | tf_op jit(solution)/shard_map/psum | solution.py:9
  300.2 0.0 copy-done
  300.2 2.4 subtract_convert_fusion
  302.5 0.0 all-gather.5.cloned.1.call-update
  302.6 48.7 %all-gather.5.cloned.1.call-done = bf16[1024,2048]{1,0:T(8,128)(2,1)} async-done(((bf16[128,2048]{1,0:T(8,128)(2,1)}), bf16[1024,2048]{1,0:T(8,128)(2,1)}) %all-gather.5.cloned.1.call-update) | async-done | bytes 4194320 | tf_op jit(solution)/shard_map/all_gather | solution.py:31
  351.3 0.0 copy-done.1
  351.3 10.8 %fusion.4 = bf16[2048,1024]{1,0:T(8,128)(2,1)} fusion(bf16[2048,1024]{1,0:T(8,128)(2,1)} %param.7, bf16[1024,2048]{1,0:T(8,128)(2,1)} %all-gather.5.cloned.1.call-done, bf16[1024,1024]{1,0:T(8,128)(2,1)S(1)} %copy-done.1), kind=kOutput, calls=%fused_computation.5 | convolution fusion | flops 4313841664 | bytes 14680064 | tf_op jit(solution)/shard_map/dot_general | solution.py:30
  (1 shorter events, 0.0 us)
Async XLA Ops:
  6.5 56.5 %all-gather.3.cloned.1.call-start = ((), (), s32[]{:S(2)}) async-start(), calls=%async_computation.1 | async-start | bytes 2162688 | tf_op jit(solution)/shard_map/all_gather | solution.py:15
  7.3 160.3 %reduce-scatter.2.cloned.1.call-start = ((), (), s32[]{:S(2)}) async-start(), calls=%async_computation.2 | async-start | bytes 9437184 | tf_op jit(solution)/shard_map/reduce_scatter | solution.py:18
  73.6 226.6 %copy-start = (s32[128]{0:T(128)S(1)}, s32[128]{0:T(128)}, u32[]{:S(2)}) copy-start(s32[128]{0:T(128)} %param.5) | copy-start | bytes 1540
  73.6 277.7 %copy-start.1 = (bf16[1024,1024]{1,0:T(8,128)(2,1)S(1)}, bf16[1024,1024]{1,0:T(8,128)(2,1)}, u32[]{:S(2)}) copy-start(bf16[1024,1024]{1,0:T(8,128)(2,1)} %all-gather.3.cloned.1.call-done) | copy-start | bytes 6291460
  73.6 277.7 %all-gather.5.cloned.1.call-start = ((), (), s32[]{:S(2)}) async-start(), calls=%async_computation.3 | async-start | bytes 4718592 | tf_op jit(solution)/shard_map/all_gather | solution.py:31
Sparse Core Ops, SparseCore 0:
  9.9 53.0 all-gather.2
  73.7 93.7 reduce-scatter.1
  302.7 48.5 all-gather.4
where the time goes:
time: 369 us
  waiting for transfers between devices  199 us (54%)
  blocking collectives  130 us (35%)
  matrix products  21.4 us (6%)
  between operations  13.1 us (4%)
  other arithmetic  5.27 us (1%)
    reduce_scatter x1, waiting for transfers between devices, local(): lax.psum_scatter(lax.dot_general(rows, head_weight, (((1,), (1,)), ((), (...  93.9 us
    psum x1, blocking collectives, softmax_by_tokens(): total = lax.psum(jnp.sum(jnp.exp(logits - peak[:, None]), axis=1), 'vocab')  67 us
    pmax x1, blocking collectives, softmax_by_tokens(): peak = lax.pmax(jnp.max(logits, axis=1), 'vocab')  62.7 us
    all_gather x1, waiting for transfers between devices, local(): all_hidden = lax.all_gather(hidden, 'vocab', axis=0, tiled=True)  55.7 us
    all_gather x1, waiting for transfers between devices, local(): lax.all_gather(resid, 'dp', axis=0, tiled=True)  48.7 us
    dot_general x1, matrix products, local(): lax.dot_general(lax.all_gather(resid, 'dp', axis=0, tiled=True), rows, ((...  10.8 us
    dot_general x1, matrix products, local(): lax.dot_general(rows, head_weight, (((1,), (1,)), ((), ())), preferred_el...  10.6 us
  transfers between devices with their start and end apart: 3, of which 3 were waited for; matrix products, arithmetic and copies ran while one was open for 0% of the time, Pallas kernels for 0%

commit v1 on v0

v1 whole, which is shorter than its diff:
```python
import functools

import jax
import jax.numpy as jnp
from jax import lax
from jax.experimental import pallas as pl
from jax.experimental.pallas import tpu as pltpu
from jax.sharding import PartitionSpec as P

MESH = pl.DeviceIdType.MESH
F32, BF16, I16 = jnp.float32, jnp.bfloat16, jnp.int16
NZ, NX, NY = 8, 4, 4
OWN = 256
HALF = 128
SB = 256
TOK = 1024
WIDTH = 1024
BLK = 32
TOP = 32760.0
TINY = 1e-30


def kernel(
    hid_ref, lab_ref, w_ref, hess_ref, out_ref,
    w_v, hess_v, h_v, lab_v, part, mb, rb, rf, bb, lg, st, st_sib, st_pl, st_z, stat, res, ob,
    loc_sem, g_send, g_recv, f_send, f_recv, lab_send, lab_recv, rs_send, rs_recv, bs_send, bs_recv,
    ag_send, ag_recv, st_send, st_recv, sib_send, sib_recv, sz_send, sz_recv, out_sem,
):
    z = lax.axis_index("dp")
    v = lax.axis_index("vocab")
    core = lax.rem(v, 2)
    chip = v // 2
    x, y = chip // NY, lax.rem(chip, NY)
    sib = (z, v + 1 - 2 * core)

    def zmod(a):
        return lax.rem(a + 2 * NZ, NZ)

    def peer(xx, yy):
        return (z, (xx * NY + yy) * 2 + core)

    def remote(src, dst, ssem, rsem, dev):
        return pltpu.make_async_remote_copy(
            src_ref=src, dst_ref=dst, send_sem=ssem, recv_sem=rsem, device_id=dev, device_id_type=MESH
        )

    w_copy = pltpu.make_async_copy(w_ref, w_v, loc_sem.at[0])
    hess_copy = pltpu.make_async_copy(hess_ref, hess_v, loc_sem.at[1])
    lab_copy = pltpu.make_async_copy(lab_ref, lab_v.at[z], loc_sem.at[2])
    w_copy.start()
    lab_copy.start()

    zring = ((zmod(z + 1), v), (zmod(z - 1), v))
    zpeers = [(zmod(z + k), v) for k in range(1, NZ)]
    plane = [peer(x, lax.rem(y + d, NY)) for d in (1, 3, 2)]
    for dx in (3, 1, 2):
        plane += [peer(lax.rem(x + dx, NX), lax.rem(y + d, NY)) for d in range(NY)]

    barrier = pltpu.get_barrier_semaphore()
    for dev in zpeers + plane + [sib]:
        pl.semaphore_signal(barrier, inc=1, device_id=dev, device_id_type=MESH)
    pl.semaphore_wait(barrier, len(zpeers) + len(plane) + 1)

    def rows(c, co):
        return h_v.at[pl.ds(pl.multiple_of((c * 2 + co) * BLK, BLK), BLK)]

    own_copy = pltpu.make_async_copy(hid_ref, rows(chip, core), g_recv.at[chip])
    own_copy.start()
    gathers = [
        remote(hid_ref, rows(chip, core), g_send.at[k], g_recv.at[chip], dev) for k, dev in enumerate(plane)
    ]
    for g in gathers:
        g.start()
    labs = [
        remote(lab_ref, lab_v.at[z], lab_send.at[k], lab_recv.at[k], dev) for k, dev in enumerate(zpeers)
    ]
    for g in labs:
        g.start()
    hess_copy.start()
    w_copy.wait()

    def xs_of(i):
        off = i + jnp.where(i == 2, 1, 0) - jnp.where(i == 3, 1, 0)
        return lax.rem(x + off, NX)

    def forward(c):
        return remote(rows(c, core), rows(c, core), f_send.at[c], f_recv.at[c], sib)

    def gather_block(xs):
        def arrive(d, _):
            c = xs * NY + lax.rem(y + d, NY)
            pltpu.make_async_copy(hid_ref, rows(c, core), g_recv.at[c]).wait()
            forward(c).start()
            return 0

        lax.fori_loop(0, NY, arrive, 0)

        def other(d, _):
            c = xs * NY + lax.rem(y + d, NY)
            remote(rows(c, 1 - core), rows(c, 1 - core), f_send.at[c], f_recv.at[c], sib).wait_recv()
            return 0

        lax.fori_loop(0, NY, other, 0)

    def mm(xs, o):
        a = w_v[pl.ds(pl.multiple_of(o * OWN, OWN), OWN), :]
        b = h_v[pl.ds(pl.multiple_of(xs * SB, SB), SB), :]
        p = lax.dot_general(a, b, (((1,), (1,)), ((), ())), preferred_element_type=F32)
        part[xs, o] = p
        mb[xs, o, 0:1, :] = jnp.max(jnp.abs(p[:HALF]), axis=0, keepdims=True)
        mb[xs, o, 1:2, :] = jnp.max(jnp.abs(p[HALF:]), axis=0, keepdims=True)

    def rows_of(xs, o, half):
        return part[xs, o, half * HALF : (half + 1) * HALF, :]

    def to_int(q):
        return jnp.round(q).astype(I16)

    def first(d, xs, place, o, half):
        b = mb[xs, o, half : half + 1, :]
        scale = TOP / jnp.maximum(b, TINY)
        rb[d, xs, 0, place * HALF : (place + 1) * HALF, :] = to_int(rows_of(xs, o, half) * scale)
        bb[d, xs, 0, place : place + 1, :] = b

    def fold(d, xs, slot, place, o, half):
        b_in = bb[d, xs, slot, place : place + 1, :]
        b = b_in + mb[xs, o, half : half + 1, :]
        inv = 1.0 / jnp.maximum(b, TINY)
        got = rb[d, xs, slot, place * HALF : (place + 1) * HALF, :].astype(F32)
        q = got * (b_in * inv) + rows_of(xs, o, half) * (TOP * inv)
        rb[d, xs, slot, place * HALF : (place + 1) * HALF, :] = to_int(q)
        bb[d, xs, slot, place : place + 1, :] = b

    def rs_data(d, xs, s):
        if s < 4:
            src, dst = rb.at[d, xs, s - 1], rb.at[d, xs, s]
        else:
            src, dst = rb.at[d, xs, 3, pl.ds(0, HALF)], rf.at[d, xs]
        return remote(src, dst, rs_send.at[d, xs, s - 1], rs_recv.at[d, xs, s - 1], zring[d])

    def rs_bound(d, xs, s):
        return remote(
            bb.at[d, xs, s - 1], bb.at[d, xs, s], bs_send.at[d, xs, s - 1], bs_recv.at[d, xs, s - 1], zring[d]
        )

    def rs_start(d, xs, s):
        rs_bound(d, xs, s).start()
        rs_data(d, xs, s).start()

    def rs_wait(d, xs, s):
        rs_bound(d, xs, s).wait_recv()
        rs_data(d, xs, s).wait_recv()

    def step1(i, _):
        xs = xs_of(i)
        gather_block(xs)

        def owners(j, _):
            mm(xs, zmod(z + 3 + j))
            return 0

        lax.fori_loop(0, 3, owners, 0)
        first(0, xs, 0, zmod(z + 4), 0)
        first(0, xs, 1, zmod(z + 3), 1)
        rs_start(0, xs, 1)
        first(1, xs, 0, zmod(z - 4), 1)
        first(1, xs, 1, zmod(z - 3), 0)
        rs_start(1, xs, 1)
        return 0

    lax.fori_loop(0, NX, step1, 0)

    for s in (1, 2):

        def step(i, _, s=s):
            xs = xs_of(i)

            def owners(j, _):
                mm(xs, zmod(z + (3 - s) * (1 - 2 * j)))
                return 0

            lax.fori_loop(0, 2, owners, 0)
            rs_wait(0, xs, s)
            fold(0, xs, s, 0, zmod(z + 4 - s), 0)
            fold(0, xs, s, 1, zmod(z + 3 - s), 1)
            rs_start(0, xs, s + 1)
            rs_wait(1, xs, s)
            fold(1, xs, s, 0, zmod(z - 4 + s), 1)
            fold(1, xs, s, 1, zmod(z - 3 + s), 0)
            rs_start(1, xs, s + 1)
            return 0

        lax.fori_loop(0, NX, step, 0)

    def step4(i, _):
        xs = xs_of(i)
        rs_wait(0, xs, 3)
        fold(0, xs, 3, 0, zmod(z + 1), 0)
        rs_start(0, xs, 4)
        rs_wait(1, xs, 3)
        fold(1, xs, 3, 0, zmod(z - 1), 1)
        rs_start(1, xs, 4)
        mm(xs, z)
        return 0

    lax.fori_loop(0, NX, step4, 0)

    def ag(d, xs, s):
        o = zmod(z + 1 - s) if d == 0 else zmod(z - 1 + s)
        ref = lg.at[o, xs]
        if s == 4:
            ref = lg.at[o, xs, pl.ds(d * HALF, HALF)]
        return remote(ref, ref, ag_send.at[d, xs, s - 1], ag_recv.at[d, xs, s - 1], zring[d])

    def ag_wait(d, xs, s):
        o = zmod(z - s) if d == 0 else zmod(z + s)
        ref = lg.at[o, xs]
        if s == 4:
            ref = lg.at[o, xs, pl.ds(d * HALF, HALF)]
        remote(ref, ref, ag_send.at[d, xs, s - 1], ag_recv.at[d, xs, s - 1], zring[d]).wait_recv()

    def total(i, _):
        xs = xs_of(i)
        rs_wait(0, xs, 4)
        rs_wait(1, xs, 4)
        b0, b1 = bb[0, xs, 4, 0:1, :], bb[1, xs, 3, 1:2, :]
        c0, c1 = bb[1, xs, 4, 0:1, :], bb[0, xs, 3, 1:2, :]
        k = 1.0 / TOP
        upper = rows_of(xs, z, 0) + rf[0, xs].astype(F32) * (b0 * k) + rb[1, xs, 3, HALF:, :].astype(F32) * (b1 * k)
        lower = rows_of(xs, z, 1) + rf[1, xs].astype(F32) * (c0 * k) + rb[0, xs, 3, HALF:, :].astype(F32) * (c1 * k)
        b = jnp.maximum(mb[xs, z, 0:1, :] + b0 + b1, mb[xs, z, 1:2, :] + c0 + c1)
        b = jnp.maximum(b, TINY)
        scale = TOP / b
        lg[z, xs, :HALF, :] = to_int(upper * scale)
        lg[z, xs, HALF:, :] = to_int(lower * scale)
        ag(0, xs, 1).start()
        ag(1, xs, 1).start()
        m = jnp.maximum(jnp.max(upper, axis=0, keepdims=True), jnp.max(lower, axis=0, keepdims=True))
        e = jnp.sum(jnp.exp(upper - m), axis=0, keepdims=True) + jnp.sum(jnp.exp(lower - m), axis=0, keepdims=True)
        for j in range(2):
            lanes = slice(128 * j, 128 * (j + 1))
            st[pl.ds(2 * xs + j, 1), :] = m[:, lanes]
            st[pl.ds(8 + 2 * xs + j, 1), :] = e[:, lanes]
            st_z[z, pl.ds(16 + 2 * xs + j, 1), :] = b[:, lanes] * k
        return 0

    lax.fori_loop(0, NX, total, 0)

    def merge(a, b):
        m = jnp.maximum(a[0], b[0])
        return m, a[1] * jnp.exp(a[0] - m) + b[1] * jnp.exp(b[0] - m)

    sib_copy = remote(st, st_sib, sib_send, sib_recv, sib)
    sib_copy.start()
    sib_copy.wait()
    m, e = merge((st[0:8], st[8:16]), (st_sib[0:8], st_sib[8:16]))
    st_pl[chip, 0:8] = m
    st_pl[chip, 8:16] = e
    spreads = [
        remote(st_pl.at[chip], st_pl.at[chip], st_send.at[k], st_recv.at[chip], dev) for k, dev in enumerate(plane)
    ]
    for g in spreads:
        g.start()

    def ag_step(s):
        def body(i, _):
            xs = xs_of(i)
            for d in (0, 1):
                ag_wait(d, xs, s)
                ag(d, xs, s + 1).start()
            return 0

        lax.fori_loop(0, NX, body, 0)

    ag_step(1)

    def plane_wait(k, _):
        c = lax.rem(chip + k, NX * NY)
        remote(st_pl.at[c], st_pl.at[c], st_send.at[0], st_recv.at[c], sib).wait_recv()
        return 0

    lax.fori_loop(1, NX * NY, plane_wait, 0)
    m = st_pl[0, 0:8]
    for c in range(1, NX * NY):
        m = jnp.maximum(m, st_pl[c, 0:8])
    e = jnp.zeros_like(m)
    for c in range(NX * NY):
        e = e + st_pl[c, 8:16] * jnp.exp(st_pl[c, 0:8] - m)
    st_z[z, 0:8] = m
    st_z[z, 8:16] = e
    deep = [remote(st_z.at[z], st_z.at[z], sz_send.at[k], sz_recv.at[k], dev) for k, dev in enumerate(zpeers)]
    for g in deep:
        g.start()

    ag_step(2)

    for k in range(NZ - 1):
        o = zmod(z - 1 - k)
        remote(st_z.at[o], st_z.at[o], sz_send.at[k], sz_recv.at[k], sib).wait_recv()
        remote(lab_v.at[o], lab_v.at[o], lab_send.at[k], lab_recv.at[k], sib).wait_recv()
    lab_copy.wait()
    m = st_z[0, 0:8]
    for o in range(1, NZ):
        m = jnp.maximum(m, st_z[o, 0:8])
    e = jnp.zeros_like(m)
    for o in range(NZ):
        e = e + st_z[o, 8:16] * jnp.exp(st_z[o, 0:8] - m)
    stat[0:8] = m
    stat[8:16] = 1.0 / e
    hess_copy.wait()

    def unit(o):
        base = v * (NZ * OWN) + o * OWN
        for r in range(8):
            top, inv = stat[r : r + 1, :], stat[8 + r : 9 + r, :]
            scale = st_z[o, 16 + r : 17 + r, :]
            lab = lab_v[r]
            lanes = slice(128 * (r % 2), 128 * (r % 2 + 1))
            for q in range(4):
                sub = slice(64 * q, 64 * (q + 1))
                l = lg[o, r // 2, sub, lanes].astype(F32) * scale
                p = jnp.exp(l - top) * inv
                ids = base + 64 * q + lax.broadcasted_iota(jnp.int32, (64, 128), 0)
                res[sub, 128 * r : 128 * (r + 1)] = (p - (ids == lab).astype(F32)).astype(BF16)

        def tile(n, _):
            cols = pl.ds(pl.multiple_of(n * 256, 256), 256)
            sums = jnp.dot(res[...], h_v[:, cols], preferred_element_type=F32)
            rws = pl.ds(pl.multiple_of(o * OWN, OWN), OWN)
            fresh = 0.9 * hess_v[rws, cols].astype(F32) + 0.1 * sums * sums
            ob[rws, cols] = jnp.clip(sums / (10000.0 * fresh), -1.0, 1.0).astype(BF16)
            return 0

        lax.fori_loop(0, WIDTH // 256, tile, 0)
        out_copy(o).start()

    def out_copy(o):
        rws = pl.ds(pl.multiple_of(o * OWN, OWN), OWN)
        return pltpu.make_async_copy(ob.at[rws], out_ref.at[rws], out_sem.at[o])

    def last(k, _):
        xs = xs_of(lax.rem(k, NX))

        @pl.when(k < NX)
        def _():
            for d in (0, 1):
                ag_wait(d, xs, 3)
                ag(d, xs, 4).start()

        @pl.when(k == 7)
        def _():
            def tail(i, _):
                for d in (0, 1):
                    ag_wait(d, xs_of(i), 4)
                return 0

            lax.fori_loop(0, NX, tail, 0)

        near = (k + 1) // 2
        unit(zmod(z + near * (1 - 2 * lax.rem(k, 2))))
        return 0

    lax.fori_loop(0, NZ, last, 0)

    for g in gathers + labs + spreads + deep:
        g.wait_send()

    def finish_gather(c, _):
        forward(c).wait_send()
        return 0

    lax.fori_loop(0, NX * NY, finish_gather, 0)

    def finish(xs, _):
        for d in (0, 1):
            for s in (1, 2, 3, 4):
                rs_data(d, xs, s).wait_send()
                rs_bound(d, xs, s).wait_send()
                ag(d, xs, s).wait_send()
        return 0

    lax.fori_loop(0, NX, finish, 0)

    def finish_out(o, _):
        out_copy(o).wait()
        return 0

    lax.fori_loop(0, NZ, finish_out, 0)


def local(hidden, labels, head_weight, hess_old):
    dma = pltpu.SemaphoreType.DMA
    return pl.pallas_call(
        kernel,
        out_shape=jax.ShapeDtypeStruct(hess_old.shape, BF16),
        in_specs=[pl.BlockSpec(memory_space=pl.ANY)] * 4,
        out_specs=pl.BlockSpec(memory_space=pl.ANY),
        scratch_shapes=[
            pltpu.VMEM((NZ * OWN, WIDTH), BF16),
            pltpu.VMEM((NZ * OWN, WIDTH), BF16),
            pltpu.VMEM((TOK, WIDTH), BF16),
            pltpu.VMEM((NZ, 1, 128), jnp.int32),
            pltpu.VMEM((NX, NZ, OWN, SB), F32),
            pltpu.VMEM((NX, NZ, 2, SB), F32),
            pltpu.VMEM((2, NX, 4, OWN, SB), I16),
            pltpu.VMEM((2, NX, HALF, SB), I16),
            pltpu.VMEM((2, NX, 5, 2, SB), F32),
            pltpu.VMEM((NZ, NX, OWN, SB), I16),
            pltpu.VMEM((16, 128), F32),
            pltpu.VMEM((16, 128), F32),
            pltpu.VMEM((NX * NY, 16, 128), F32),
            pltpu.VMEM((NZ, 24, 128), F32),
            pltpu.VMEM((16, 128), F32),
            pltpu.VMEM((OWN, TOK), BF16),
            pltpu.VMEM((NZ * OWN, WIDTH), BF16),
            dma((3,)),
            dma((15,)), dma((16,)), dma((16,)), dma((16,)),
            dma((7,)), dma((7,)),
            dma((2, NX, 4)), dma((2, NX, 4)),
            dma((2, NX, 4)), dma((2, NX, 4)),
            dma((2, NX, 4)), dma((2, NX, 4)),
            dma((15,)), dma((16,)),
            dma, dma,
            dma((7,)), dma((7,)),
            dma((NZ,)),
        ],
        compiler_params=pltpu.CompilerParams(
            collective_id=0, has_side_effects=True, vmem_limit_bytes=56 * 2**20
        ),
        cost_estimate=pl.CostEstimate(
            flops=8 * TOK * NZ * OWN * WIDTH, bytes_accessed=13 * 2**20, transcendentals=TOK * NZ * OWN
        ),
    )(hidden, labels.reshape(1, 128), head_weight, hess_old)


def solution(mesh):
    in_specs = (P("vocab", "dp"), P("dp"), P("vocab", "dp"), P("vocab", "dp"))
    out_specs = P("vocab", "dp")
    return jax.shard_map(local, mesh=mesh, in_specs=in_specs, out_specs=out_specs, check_vma=False)
```

time: 369 us -> 121 us (0.33)
  waiting for transfers between devices: 199 us -> 0 us
  blocking collectives: 130 us -> 0 us
  Pallas kernels: 0 us -> 116 us
  matrix products: 21.4 us -> 0 us
  between operations: 13.1 us -> 0.01 us
  other arithmetic: 5.27 us -> 0 us
  local copies, waits for them, and re-layouts: 0.01 us -> 4.64 us
    pallas_call x0 -> x1, Pallas kernels: none -> 116 us  [local(): pl.pallas_call(kernel, out_shape=jax.ShapeDtypeStruct(hess_old.shape, BF1...]
    all_gather x2 -> x0, waiting for transfers between devices: 104 us -> none  [the longest x1 55.7 us: local(): all_hidden = lax.all_gather(hidden, 'vocab', axis=0, tiled=True)]
    reduce_scatter x1 -> x0, waiting for transfers between devices: 93.9 us -> none  [local(): lax.psum_scatter(lax.dot_general(rows, head_weight, (((1,), (1,)), ((), (...]
    psum x1 -> x0, blocking collectives: 67 us -> none  [softmax_by_tokens(): total = lax.psum(jnp.sum(jnp.exp(logits - peak[:, None]), axis=1), 'vocab')]
    pmax x1 -> x0, blocking collectives: 62.7 us -> none  [softmax_by_tokens(): peak = lax.pmax(jnp.max(logits, axis=1), 'vocab')]
    dot_general x2 -> x0, matrix products: 21.4 us -> none  [the longest x1 10.8 us: local(): lax.dot_general(lax.all_gather(resid, 'dp', axis=0, tiled=True), rows, ((...]
    unnamed x4 -> x1, local copies, waits for them, and re-layouts: 0.01 us -> 4.64 us
  transfers between devices with their start and end apart: 3 -> 0, of which waited for: 3 -> 0; matrix products, arithmetic and copies ran while one was open for 0% -> 0% of each run, Pallas kernels for 0% -> 0%
where the time goes in v1:
time: 121 us
  Pallas kernels  116 us (96%)
  local copies, waits for them, and re-layouts  4.64 us (4%)
    pallas_call x1, Pallas kernels, local(): pl.pallas_call(kernel, out_shape=jax.ShapeDtypeStruct(hess_old.shape, BF1...  116 us
    unnamed x1, local copies, waits for them, and re-layouts  4.64 us

profile of v1, /device:TPU:1, one launch (start us, length us, event | category | flops | bytes accessed | tf_op | source)
XLA Modules:
  0.0 121.1 jit_solution(8213707328643752709)
XLA Ops:
  0.0 116.5 %shard_map.46 = bf16[2048,1024]{1,0:T(8,128)(2,1)} custom-call(bf16[32,1024]{1,0:T(8,128)(2,1)} %hid_ref.1, s32[1,128]{1,0:T(1,128)} %bitcast.1, bf16[2048,1024]{1,0:T(8,128)(2,1)} %w_ref.1, bf16[2048,1024]{1,0:T(8,128)(2,1)} %hess_ref.1), custom_call_target="tpu_custom_call" | custom-call | flops 17179869184 | bytes 13631488 | tf_op jit(solution)/shard_map/pallas_call | solution.py:393
  116.5 4.6 %copy.6 = bf16[2048,1024]{1,0:T(8,128)(2,1)} copy(bf16[2048,1024]{1,0:T(8,128)(2,1)} %shard_map.46) | data formatting | bytes 8388608

commit v2 on v1

v2 whole, which is shorter than its diff:
```python
import functools

import jax
import jax.numpy as jnp
from jax import lax
from jax.experimental import pallas as pl
from jax.experimental.pallas import tpu as pltpu
from jax.sharding import PartitionSpec as P

MESH = pl.DeviceIdType.MESH
F32, BF16, I16 = jnp.float32, jnp.bfloat16, jnp.int16
NZ, NX, NY = 8, 4, 4
OWN = 256
HALF = 128
SB = 256
TOK = 1024
WIDTH = 1024
BLK = 32
TOP = 32760.0
TINY = 1e-30
SLOTS = (
    (0, 0), (0, 1), (0, 3), (1, 0),
    (3, 0), (1, 1), (3, 3), (1, 3),
    (3, 1), (2, 0), (0, 2), (2, 1),
    (2, 3), (1, 2), (3, 2), (2, 2),
)
HOPS = {
    0: ((1, (0, 1)), (2, (0, 3)), (3, (1, 0)), (4, (3, 0))),
    1: ((8, (3, 0)), (10, (0, 1))),
    2: ((7, (1, 0)),),
    3: ((5, (0, 1)), (9, (1, 0))),
    4: ((6, (0, 3)),),
    5: ((11, (1, 0)),),
    6: ((12, (3, 0)),),
    7: ((13, (0, 3)),),
    8: ((14, (0, 1)),),
    14: ((15, (3, 0)),),
}
ARRIVE = ((1, 2, 3, 4), (5, 6, 7, 8, 9, 10), (11, 12, 13, 14), (15,))
ORDER = ((1, 0), (1, 1), (2, 0), (1, 2), (2, 1), (1, 3), (2, 2), (3, 0), (2, 3), (3, 1), (3, 2), (3, 3))


def pick(k, values):
    out = values[0]
    for j in range(1, len(values)):
        out = jnp.where(k == j, values[j], out)
    return out


def kernel(
    hid_ref, lab_ref, w_ref, hess_ref, out_ref,
    w_v, hess_v, h_v, lab_v, lab_t, lab_l, part, mb, rb, rf, bb, lg, st_l, st, st_f, st_sib, st_y, st_x, st_z, stat, res,
    loc_sem, g_send, g_recv, f_send, f_recv, lab_send, lab_recv, rs_send, rs_recv, bs_send, bs_recv,
    ag_send, ag_recv, sy_send, sy_recv, sx_send, sx_recv, sib_send, sib_recv, sz_send, sz_recv,
):
    z = lax.axis_index("dp")
    v = lax.axis_index("vocab")
    core = lax.rem(v, 2)
    chip = v // 2
    x, y = chip // NY, lax.rem(chip, NY)
    sib = (z, v + 1 - 2 * core)

    def zmod(a):
        return lax.rem(a + 2 * NZ, NZ)

    def at(dx, dy):
        return (z, (lax.rem(x + dx, NX) * NY + lax.rem(y + dy, NY)) * 2 + core)

    def chip_of(k):
        dx, dy = SLOTS[k]
        return lax.rem(x + NX - dx, NX) * NY + lax.rem(y + NY - dy, NY)

    def remote(src, dst, ssem, rsem, dev):
        return pltpu.make_async_remote_copy(
            src_ref=src, dst_ref=dst, send_sem=ssem, recv_sem=rsem, device_id=dev, device_id_type=MESH
        )

    w_copy = pltpu.make_async_copy(w_ref, w_v, loc_sem.at[0])
    hess_copy = pltpu.make_async_copy(hess_ref, hess_v, loc_sem.at[1])
    lab_copy = pltpu.make_async_copy(lab_ref, lab_v.at[z], loc_sem.at[2])

    def slot(k, co):
        return h_v.at[pl.ds(pl.multiple_of(k * 2 * BLK + co * BLK, BLK), BLK)]

    own_copy = pltpu.make_async_copy(hid_ref, slot(0, core), loc_sem.at[3])
    w_copy.start()
    lab_copy.start()
    own_copy.start()

    zring = ((zmod(z + 1), v), (zmod(z - 1), v))
    zpeers = [(zmod(z + k), v) for k in range(1, NZ)]
    ypeers = [at(0, d) for d in range(1, NY)]
    xpeers = [at(d, 0) for d in range(1, NX)]

    barrier = pltpu.get_barrier_semaphore()
    partners = zpeers + ypeers + xpeers + [sib]
    for dev in partners:
        pl.semaphore_signal(barrier, inc=1, device_id=dev, device_id_type=MESH)
    pl.semaphore_wait(barrier, len(partners))

    def hop(k, c, step):
        src = hid_ref if k == 0 else slot(k, core)
        return remote(src, slot(c, core), g_send.at[c], g_recv.at[c], at(*step))

    def share(k):
        src = hid_ref if k == 0 else slot(k, core)
        return remote(src, slot(k, core), f_send.at[k], f_recv.at[k], sib)

    for c, step in HOPS[0]:
        hop(0, c, step).start()
    share(0).start()
    labs = [
        remote(lab_ref, lab_v.at[z], lab_send.at[k], lab_recv.at[k], dev) for k, dev in enumerate(zpeers)
    ]
    for g in labs:
        g.start()
    hess_copy.start()
    own_copy.wait()
    w_copy.wait()

    def gather_group(i):
        for k in ARRIVE[i]:
            remote(slot(k, core), slot(k, core), g_send.at[k], g_recv.at[k], sib).wait_recv()
            for c, step in HOPS.get(k, ()):
                hop(k, c, step).start()
            share(k).start()
        for k in range(4 * i, 4 * i + 4):
            remote(slot(k, 1 - core), slot(k, 1 - core), f_send.at[k], f_recv.at[k], sib).wait_recv()

    def mm(xs, o):
        a = w_v[pl.ds(pl.multiple_of(o * OWN, OWN), OWN), :]
        b = h_v[pl.ds(pl.multiple_of(xs * SB, SB), SB), :]
        p = lax.dot_general(a, b, (((1,), (1,)), ((), ())), preferred_element_type=F32)
        part[xs, o] = p
        mb[xs, o, 0:1, :] = jnp.max(jnp.abs(p[:HALF]), axis=0, keepdims=True)
        mb[xs, o, 1:2, :] = jnp.max(jnp.abs(p[HALF:]), axis=0, keepdims=True)

    def rows_of(xs, o, half):
        return part[xs, o, half * HALF : (half + 1) * HALF, :]

    def to_int(q):
        return jnp.round(q).astype(I16)

    def first(d, xs, place, o, half):
        b = mb[xs, o, half : half + 1, :]
        scale = TOP / jnp.maximum(b, TINY)
        rb[d, xs, 0, place * HALF : (place + 1) * HALF, :] = to_int(rows_of(xs, o, half) * scale)
        bb[d, xs, 0, place : place + 1, :] = b

    def fold(d, xs, slot, place, o, half):
        b_in = bb[d, xs, slot, place : place + 1, :]
        b = b_in + mb[xs, o, half : half + 1, :]
        inv = 1.0 / jnp.maximum(b, TINY)
        got = rb[d, xs, slot, place * HALF : (place + 1) * HALF, :].astype(F32)
        q = got * (b_in * inv) + rows_of(xs, o, half) * (TOP * inv)
        rb[d, xs, slot, place * HALF : (place + 1) * HALF, :] = to_int(q)
        bb[d, xs, slot, place : place + 1, :] = b

    def rs_data(d, xs, s):
        if not isinstance(s, int) or s < 4:
            src, dst = rb.at[d, xs, s - 1], rb.at[d, xs, s]
        else:
            src, dst = rb.at[d, xs, 3, pl.ds(0, HALF)], rf.at[d, xs]
        return remote(src, dst, rs_send.at[d, xs, s - 1], rs_recv.at[d, xs, s - 1], zring[d])

    def rs_bound(d, xs, s):
        return remote(
            bb.at[d, xs, s - 1], bb.at[d, xs, s], bs_send.at[d, xs, s - 1], bs_recv.at[d, xs, s - 1], zring[d]
        )

    def rs_start(d, xs, s):
        rs_bound(d, xs, s).start()
        rs_data(d, xs, s).start()

    def rs_wait(d, xs, s):
        rs_bound(d, xs, s).wait_recv()
        rs_data(d, xs, s).wait_recv()

    def event(k, _):
        s = pick(k, [e[0] for e in ORDER])
        i = pick(k, [e[1] for e in ORDER])

        for g in range(4):

            @pl.when((s == 1) & (i == g))
            def _(g=g):
                gather_group(g)

        @pl.when(s == 1)
        def _():
            def owners(j, _):
                mm(i, zmod(z + 3 + j))
                return 0

            lax.fori_loop(0, 3, owners, 0)
            first(0, i, 0, zmod(z + 4), 0)
            first(0, i, 1, zmod(z + 3), 1)
            rs_start(0, i, 1)
            first(1, i, 0, zmod(z - 4), 1)
            first(1, i, 1, zmod(z - 3), 0)
            rs_start(1, i, 1)

        @pl.when(s > 1)
        def _():
            def owners(j, _):
                mm(i, zmod(z + (4 - s) * (1 - 2 * j)))
                return 0

            lax.fori_loop(0, 2, owners, 0)
            rs_wait(0, i, s - 1)
            fold(0, i, s - 1, 0, zmod(z + 5 - s), 0)
            fold(0, i, s - 1, 1, zmod(z + 4 - s), 1)
            rs_start(0, i, s)
            rs_wait(1, i, s - 1)
            fold(1, i, s - 1, 0, zmod(z - 5 + s), 1)
            fold(1, i, s - 1, 1, zmod(z - 4 + s), 0)
            rs_start(1, i, s)

        return 0

    lax.fori_loop(0, len(ORDER), event, 0)

    def step4(i, _):
        xs = i
        rs_wait(0, xs, 3)
        fold(0, xs, 3, 0, zmod(z + 1), 0)
        rs_start(0, xs, 4)
        rs_wait(1, xs, 3)
        fold(1, xs, 3, 0, zmod(z - 1), 1)
        rs_start(1, xs, 4)
        mm(xs, z)
        return 0

    lax.fori_loop(0, NX, step4, 0)

    def ag(d, xs, s):
        o = zmod(z + 1 - s) if d == 0 else zmod(z - 1 + s)
        ref = lg.at[o, xs]
        if s == 4:
            ref = lg.at[o, xs, pl.ds(d * HALF, HALF)]
        return remote(ref, ref, ag_send.at[d, xs, s - 1], ag_recv.at[d, xs, s - 1], zring[d])

    def ag_wait(d, xs, s):
        o = zmod(z - s) if d == 0 else zmod(z + s)
        ref = lg.at[o, xs]
        if s == 4:
            ref = lg.at[o, xs, pl.ds(d * HALF, HALF)]
        remote(ref, ref, ag_send.at[d, xs, s - 1], ag_recv.at[d, xs, s - 1], zring[d]).wait_recv()

    def total(i, _):
        xs = i
        rs_wait(0, xs, 4)
        rs_wait(1, xs, 4)
        b0, b1 = bb[0, xs, 4, 0:1, :], bb[1, xs, 3, 1:2, :]
        c0, c1 = bb[1, xs, 4, 0:1, :], bb[0, xs, 3, 1:2, :]
        k = 1.0 / TOP
        upper = rows_of(xs, z, 0) + rf[0, xs].astype(F32) * (b0 * k) + rb[1, xs, 3, HALF:, :].astype(F32) * (b1 * k)
        lower = rows_of(xs, z, 1) + rf[1, xs].astype(F32) * (c0 * k) + rb[0, xs, 3, HALF:, :].astype(F32) * (c1 * k)
        b = jnp.maximum(mb[xs, z, 0:1, :] + b0 + b1, mb[xs, z, 1:2, :] + c0 + c1)
        b = jnp.maximum(b, TINY)
        scale = TOP / b
        lg[z, xs, :HALF, :] = to_int(upper * scale)
        lg[z, xs, HALF:, :] = to_int(lower * scale)
        ag(0, xs, 1).start()
        ag(1, xs, 1).start()
        m = jnp.maximum(jnp.max(upper, axis=0, keepdims=True), jnp.max(lower, axis=0, keepdims=True))
        e = jnp.sum(jnp.exp(upper - m), axis=0, keepdims=True) + jnp.sum(jnp.exp(lower - m), axis=0, keepdims=True)
        for j in range(2):
            lanes = slice(128 * j, 128 * (j + 1))
            st_l[pl.ds(2 * xs + j, 1), :] = m[:, lanes]
            st_l[pl.ds(8 + 2 * xs + j, 1), :] = e[:, lanes]
            st_z[z, pl.ds(16 + 2 * xs + j, 1), :] = b[:, lanes] * k
        return 0

    lax.fori_loop(0, NX, total, 0)

    left8 = lax.broadcasted_iota(jnp.int32, (8, 128), 1) < 64
    left16 = lax.broadcasted_iota(jnp.int32, (16, 128), 1) < 64

    def swap(a):
        return pltpu.roll(a, 64, 1)

    def merge(parts):
        m = parts[0]
        for a in parts[1:]:
            m = jnp.maximum(m, a)
        e = jnp.zeros_like(m)
        for a in parts:
            e = e + a * swap(jnp.exp(a - m))
        return jnp.where(left16, m, e)

    m, e = st_l[0:8], st_l[8:16]
    even, odd = jnp.where(left8, m, swap(e)), jnp.where(left8, swap(m), e)
    for r in range(8):
        st[pl.ds(chip_of(2 * r), 1), :] = even[r : r + 1]
        st[pl.ds(chip_of(2 * r + 1), 1), :] = odd[r : r + 1]

    sib_copy = remote(st, st_sib, sib_send, sib_recv, sib)
    ycopies = [remote(st_y.at[0], st_y.at[d], sy_send.at[d], sy_recv.at[d], ypeers[d - 1]) for d in range(1, NY)]
    xcopies = [remote(st_x.at[0], st_x.at[d], sx_send.at[d], sx_recv.at[d], xpeers[d - 1]) for d in range(1, NX)]
    zcopies = [remote(st_z.at[z], st_z.at[z], sz_send.at[k], sz_recv.at[k], dev) for k, dev in enumerate(zpeers)]
    sib_copy.start()
    sib_copy.wait_recv()
    st_y[0] = merge([st[...], st_sib[...]])
    for g in ycopies:
        g.start()

    def ag_next(i, s):
        for d in (0, 1):
            ag_wait(d, i, s - 1)
            ag(d, i, s).start()

    def ag_two(i, _):
        ag_next(i, 2)

        @pl.when(i == 1)
        def _():
            for g in ycopies:
                g.wait_recv()
            st_x[0] = merge([st_y[d] for d in range(NY)])
            for g in xcopies:
                g.start()

        @pl.when(i == 3)
        def _():
            for g in xcopies:
                g.wait_recv()
            st_z[z, 0:16] = merge([st_x[d] for d in range(NX)])
            for g in zcopies:
                g.start()

        return 0

    lax.fori_loop(0, NX, ag_two, 0)

    def settle():
        for k in range(NZ - 1):
            o = zmod(z - 1 - k)
            remote(st_z.at[o], st_z.at[o], sz_send.at[k], sz_recv.at[k], sib).wait_recv()
            remote(lab_v.at[o], lab_v.at[o], lab_send.at[k], lab_recv.at[k], sib).wait_recv()
        lab_copy.wait()
        hess_copy.wait()
        st_f[...] = merge([st_z[o, 0:16] for o in range(NZ)])
        for r in range(8):
            lab_t[r : r + 1, :] = lab_v[r]
        lab_t[8:16] = swap(lab_t[0:8])
        for r in range(8):
            a, b = chip_of(2 * r), chip_of(2 * r + 1)
            st_l[r : r + 1, :] = st_f[pl.ds(a, 1), :]
            st_l[8 + r : 9 + r, :] = st_f[pl.ds(b, 1), :]
            lab_l[r : r + 1, :] = jnp.where(
                left8[0:1], lab_t[pl.ds(a // 2 + 8 * lax.rem(a, 2), 1), :], lab_t[pl.ds(b // 2 + 8 * (1 - lax.rem(b, 2)), 1), :]
            )
        a, b = st_l[0:8], st_l[8:16]
        stat[0:8] = jnp.where(left8, a, swap(b))
        stat[8:16] = 1.0 / jnp.where(left8, swap(a), b)

    def prep(o, i):
        base = v * (NZ * OWN) + o * OWN
        for h in range(2):
            r = 2 * i + h
            top, inv = stat[pl.ds(r, 1), :], stat[pl.ds(8 + r, 1), :]
            scale = st_z[o, pl.ds(16 + r, 1), :]
            lab = lab_l[pl.ds(r, 1), :]
            for q in range(4):
                sub = slice(64 * q, 64 * (q + 1))
                l = lg[o, i, sub, 128 * h : 128 * (h + 1)].astype(F32) * scale
                p = jnp.exp(l - top) * inv
                ids = base + 64 * q + lax.broadcasted_iota(jnp.int32, (64, 128), 0)
                lanes = pl.ds(pl.multiple_of(256 * i + 128 * h, 128), 128)
                res[sub, lanes] = (p - (ids == lab).astype(F32)).astype(BF16)

    def tile(o, n):
        cols = pl.ds(pl.multiple_of(n * 256, 256), 256)
        sums = jnp.dot(res[...], h_v[:, cols], preferred_element_type=F32)
        rws = pl.ds(pl.multiple_of(o * OWN, OWN), OWN)
        fresh = 0.9 * hess_v[rws, cols].astype(F32) + 0.1 * sums * sums
        out_ref[rws, cols] = jnp.clip(sums / (10000.0 * fresh), -1.0, 1.0).astype(BF16)

    def last(k, _):
        @pl.when(k < NX)
        def _():
            ag_next(k, 3)

        @pl.when(k == 0)
        def _():
            settle()

        @pl.when((k >= NX) & (k < 2 * NX))
        def _():
            ag_next(k - NX, 4)

        u = jnp.where(k < 6, k - 1, k - 3)
        o = zmod(z + ((u + 1) // 2) * (1 - 2 * lax.rem(u + 2, 2)))

        @pl.when(((k >= 1) & (k < 6)) | (k >= 8))
        def _():
            def preps(i, _):
                @pl.when(k == 10)
                def _():
                    for d in (0, 1):
                        ag_wait(d, i, 4)

                prep(o, i)
                return 0

            lax.fori_loop(0, NX, preps, 0)

            def tiles(n, _):
                tile(o, n)
                return 0

            lax.fori_loop(0, WIDTH // 256, tiles, 0)

        return 0

    lax.fori_loop(0, 11, last, 0)

    for c in range(1, 16):
        remote(slot(c, core), slot(c, core), g_send.at[c], g_recv.at[c], sib).wait_send()
    for k in range(16):
        share(k).wait_send()
    for g in labs + [sib_copy] + ycopies + xcopies + zcopies:
        g.wait_send()

    def finish(xs, _):
        for d in (0, 1):
            for s in (1, 2, 3, 4):
                rs_data(d, xs, s).wait_send()
                rs_bound(d, xs, s).wait_send()
                ag(d, xs, s).wait_send()
        return 0

    lax.fori_loop(0, NX, finish, 0)


def local(hidden, labels, head_weight, hess_old):
    dma = pltpu.SemaphoreType.DMA
    return pl.pallas_call(
        kernel,
        out_shape=pltpu.VMEM(hess_old.shape, BF16),
        in_specs=[pl.BlockSpec(memory_space=pl.ANY)] * 4,
        out_specs=pl.BlockSpec(memory_space=pltpu.VMEM),
        scratch_shapes=[
            pltpu.VMEM((NZ * OWN, WIDTH), BF16),
            pltpu.VMEM((NZ * OWN, WIDTH), BF16),
            pltpu.VMEM((TOK, WIDTH), BF16),
            pltpu.VMEM((NZ, 1, 128), jnp.int32),
            pltpu.VMEM((16, 128), jnp.int32),
            pltpu.VMEM((8, 128), jnp.int32),
            pltpu.VMEM((NX, NZ, OWN, SB), F32),
            pltpu.VMEM((NX, NZ, 2, SB), F32),
            pltpu.VMEM((2, NX, 4, OWN, SB), I16),
            pltpu.VMEM((2, NX, HALF, SB), I16),
            pltpu.VMEM((2, NX, 5, 2, SB), F32),
            pltpu.VMEM((NZ, NX, OWN, SB), I16),
            pltpu.VMEM((16, 128), F32),
            pltpu.VMEM((16, 128), F32),
            pltpu.VMEM((16, 128), F32),
            pltpu.VMEM((16, 128), F32),
            pltpu.VMEM((NY, 16, 128), F32),
            pltpu.VMEM((NX, 16, 128), F32),
            pltpu.VMEM((NZ, 24, 128), F32),
            pltpu.VMEM((16, 128), F32),
            pltpu.VMEM((OWN, TOK), BF16),
            dma((4,)),
            dma((16,)), dma((16,)), dma((16,)), dma((16,)),
            dma((7,)), dma((7,)),
            dma((2, NX, 4)), dma((2, NX, 4)),
            dma((2, NX, 4)), dma((2, NX, 4)),
            dma((2, NX, 4)), dma((2, NX, 4)),
            dma((NY,)), dma((NY,)),
            dma((NX,)), dma((NX,)),
            dma, dma,
            dma((7,)), dma((7,)),
        ],
        compiler_params=pltpu.CompilerParams(
            collective_id=0, has_side_effects=True, vmem_limit_bytes=56 * 2**20
        ),
        cost_estimate=pl.CostEstimate(
            flops=8 * TOK * NZ * OWN * WIDTH, bytes_accessed=13 * 2**20, transcendentals=TOK * NZ * OWN
        ),
    )(hidden, labels.reshape(1, 128), head_weight, hess_old)


def solution(mesh):
    in_specs = (P("vocab", "dp"), P("dp"), P("vocab", "dp"), P("vocab", "dp"))
    out_specs = P("vocab", "dp")
    return jax.shard_map(local, mesh=mesh, in_specs=in_specs, out_specs=out_specs, check_vma=False)
```

time: 121 us -> 109 us (0.901)
  Pallas kernels: 116 us -> 107 us
  local copies, waits for them, and re-layouts: 4.64 us -> 2.02 us
    pallas_call x1, Pallas kernels: 116 us -> 107 us  [local(): pl.pallas_call(kernel, out_shape=pltpu.VMEM(hess_old.shape, BF16), in_spe...]
    unnamed x1, local copies, waits for them, and re-layouts: 4.64 us -> 2.02 us
where the time goes in v2:
time: 109 us
  Pallas kernels  107 us (98%)
  local copies, waits for them, and re-layouts  2.02 us (2%)
    pallas_call x1, Pallas kernels, local(): pl.pallas_call(kernel, out_shape=pltpu.VMEM(hess_old.shape, BF16), in_spe...  107 us

profile of v2, /device:TPU:1, one launch (start us, length us, event | category | flops | bytes accessed | tf_op | source)
XLA Modules:
  0.0 108.6 jit_solution(10954597648542185745)
XLA Ops:
  0.0 106.6 %shard_map.46 = bf16[2048,1024]{1,0:T(8,128)(2,1)S(1)} custom-call(bf16[32,1024]{1,0:T(8,128)(2,1)} %hid_ref.1, s32[1,128]{1,0:T(1,128)} %bitcast.1, bf16[2048,1024]{1,0:T(8,128)(2,1)} %w_ref.1, bf16[2048,1024]{1,0:T(8,128)(2,1)} %hess_ref.1), custom_call_target="tpu_custom_call" | custom-call | flops 17179869184 | bytes 13631488 | tf_op jit(solution)/shard_map/pallas_call | solution.py:439
  106.6 2.0 %copy.6 = bf16[2048,1024]{1,0:T(8,128)(2,1)} copy(bf16[2048,1024]{1,0:T(8,128)(2,1)S(1)} %shard_map.46) | data formatting | bytes 8388608

commit v3 on v2

--- a/solution.py
+++ b/solution.py
@@ -25,18 +25,19 @@
     (2, 3), (1, 2), (3, 2), (2, 2),
 )
 HOPS = {
-    0: ((1, (0, 1)), (2, (0, 3)), (3, (1, 0)), (4, (3, 0))),
-    1: ((8, (3, 0)), (10, (0, 1))),
-    2: ((7, (1, 0)),),
-    3: ((5, (0, 1)), (9, (1, 0))),
-    4: ((6, (0, 3)),),
+    0: (
+        (1, (0, 1)), (2, (0, 3)), (3, (1, 0)), (4, (3, 0)),
+        (5, (1, 1)), (6, (3, 3)), (7, (1, 3)), (8, (3, 1)),
+    ),
+    1: ((10, (0, 1)),),
+    3: ((9, (1, 0)),),
     5: ((11, (1, 0)),),
     6: ((12, (3, 0)),),
     7: ((13, (0, 3)),),
     8: ((14, (0, 1)),),
     14: ((15, (3, 0)),),
 }
-ARRIVE = ((1, 2, 3, 4), (5, 6, 7, 8, 9, 10), (11, 12, 13, 14), (15,))
+ARRIVE = ((1, 2, 3, 4), (5, 6, 7, 8), (9, 10, 11, 12, 13, 14), (15,))
 ORDER = ((1, 0), (1, 1), (2, 0), (1, 2), (2, 1), (1, 3), (2, 2), (3, 0), (2, 3), (3, 1), (3, 2), (3, 3))
 
 
@@ -47,9 +48,14 @@
     return out
 
 
+def step_of(sums, old):
+    fresh = 0.9 * old.astype(F32) + 0.1 * sums * sums
+    return jnp.clip(sums / (10000.0 * fresh), -1.0, 1.0).astype(BF16)
+
+
 def kernel(
-    hid_ref, lab_ref, w_ref, hess_ref, out_ref,
-    w_v, hess_v, h_v, lab_v, lab_t, lab_l, part, mb, rb, rf, bb, lg, st_l, st, st_f, st_sib, st_y, st_x, st_z, stat, res,
+    hid_ref, lab_ref, w_ref, hess_ref, out_ref, res, h_v, hess_l,
+    w_v, hess_v, lab_v, lab_t, lab_l, part, mb, rb, rf, bb, lg, st_l, st, st_f, st_sib, st_y, st_x, st_z, stat,
     loc_sem, g_send, g_recv, f_send, f_recv, lab_send, lab_recv, rs_send, rs_recv, bs_send, bs_recv,
     ag_send, ag_recv, sy_send, sy_recv, sx_send, sx_recv, sib_send, sib_recv, sz_send, sz_recv,
 ):
@@ -82,6 +88,8 @@
     def slot(k, co):
         return h_v.at[pl.ds(pl.multiple_of(k * 2 * BLK + co * BLK, BLK), BLK)]
 
+    far = pl.ds(pl.multiple_of(zmod(z + 4) * OWN, OWN), OWN)
+    far_copy = pltpu.make_async_copy(hess_ref.at[far], hess_l, loc_sem.at[4])
     own_copy = pltpu.make_async_copy(hid_ref, slot(0, core), loc_sem.at[3])
     w_copy.start()
     lab_copy.start()
@@ -93,7 +101,8 @@
     xpeers = [at(d, 0) for d in range(1, NX)]
 
     barrier = pltpu.get_barrier_semaphore()
-    partners = zpeers + ypeers + xpeers + [sib]
+    partners = list(zring) + [at(0, 1), at(0, 3), at(1, 0), at(3, 0), sib]
+    partners += [at(dx, dy) for dx in (1, 3) for dy in (1, 3)]
     for dev in partners:
         pl.semaphore_signal(barrier, inc=1, device_id=dev, device_id_type=MESH)
     pl.semaphore_wait(barrier, len(partners))
@@ -106,17 +115,22 @@
         src = hid_ref if k == 0 else slot(k, core)
         return remote(src, slot(k, core), f_send.at[k], f_recv.at[k], sib)
 
-    for c, step in HOPS[0]:
+    for c, step in HOPS[0][:4]:
         hop(0, c, step).start()
     share(0).start()
-    labs = [
-        remote(lab_ref, lab_v.at[z], lab_send.at[k], lab_recv.at[k], dev) for k, dev in enumerate(zpeers)
-    ]
-    for g in labs:
-        g.start()
-    hess_copy.start()
+    def lab_hop(d, step):
+        o = zmod(z + 1 - step) if d == 0 else zmod(z - 1 + step)
+        return remote(lab_v.at[o], lab_v.at[o], lab_send.at[d, step - 1], lab_recv.at[d, step - 1], zring[d])
+
+    lab_copy.wait()
+    for d in (0, 1):
+        lab_hop(d, 1).start()
     own_copy.wait()
     w_copy.wait()
+    for c, step in HOPS[0][:4]:
+        hop(0, c, step).wait_send()
+    for c, step in HOPS[0][4:]:
+        hop(0, c, step).start()
 
     def gather_group(i):
         for k in ARRIVE[i]:
@@ -192,10 +206,11 @@
                 mm(i, zmod(z + 3 + j))
                 return 0
 
-            lax.fori_loop(0, 3, owners, 0)
+            lax.fori_loop(0, 2, owners, 0)
             first(0, i, 0, zmod(z + 4), 0)
             first(0, i, 1, zmod(z + 3), 1)
             rs_start(0, i, 1)
+            lax.fori_loop(2, 3, owners, 0)
             first(1, i, 0, zmod(z - 4), 1)
             first(1, i, 1, zmod(z - 3), 0)
             rs_start(1, i, 1)
@@ -216,9 +231,21 @@
             fold(1, i, s - 1, 1, zmod(z - 4 + s), 0)
             rs_start(1, i, s)
 
+        for step in (1, 2, 3):
+
+            @pl.when(k == 3 * step)
+            def _(step=step):
+                for d in (0, 1):
+                    lab_hop(d, step).wait_recv()
+                    if step < 3 or d == 0:
+                        lab_hop(d, step + 1).start()
+
         return 0
 
     lax.fori_loop(0, len(ORDER), event, 0)
+
+    hess_copy.start()
+    far_copy.start()
 
     def step4(i, _):
         xs = i
@@ -337,9 +364,9 @@
         for k in range(NZ - 1):
             o = zmod(z - 1 - k)
             remote(st_z.at[o], st_z.at[o], sz_send.at[k], sz_recv.at[k], sib).wait_recv()
-            remote(lab_v.at[o], lab_v.at[o], lab_send.at[k], lab_recv.at[k], sib).wait_recv()
-        lab_copy.wait()
+        lab_hop(0, 4).wait_recv()
         hess_copy.wait()
+        far_copy.wait()
         st_f[...] = merge([st_z[o, 0:16] for o in range(NZ)])
         for r in range(8):
             lab_t[r : r + 1, :] = lab_v[r]
@@ -372,10 +399,9 @@
 
     def tile(o, n):
         cols = pl.ds(pl.multiple_of(n * 256, 256), 256)
+        rws = pl.ds(pl.multiple_of(o * OWN, OWN), OWN)
         sums = jnp.dot(res[...], h_v[:, cols], preferred_element_type=F32)
-        rws = pl.ds(pl.multiple_of(o * OWN, OWN), OWN)
-        fresh = 0.9 * hess_v[rws, cols].astype(F32) + 0.1 * sums * sums
-        out_ref[rws, cols] = jnp.clip(sums / (10000.0 * fresh), -1.0, 1.0).astype(BF16)
+        out_ref[rws, cols] = step_of(sums, hess_v[rws, cols])
 
     def last(k, _):
         @pl.when(k < NX)
@@ -410,18 +436,24 @@
                 tile(o, n)
                 return 0
 
-            lax.fori_loop(0, WIDTH // 256, tiles, 0)
+            @pl.when(k < 10)
+            def _():
+                lax.fori_loop(0, WIDTH // 256, tiles, 0)
 
         return 0
 
     lax.fori_loop(0, 11, last, 0)
 
-    for c in range(1, 16):
+    for c in range(5, 16):
         remote(slot(c, core), slot(c, core), g_send.at[c], g_recv.at[c], sib).wait_send()
     for k in range(16):
         share(k).wait_send()
-    for g in labs + [sib_copy] + ycopies + xcopies + zcopies:
+    for g in [sib_copy] + ycopies + xcopies + zcopies:
         g.wait_send()
+    for step in (1, 2, 3, 4):
+        for d in (0, 1):
+            if step < 4 or d == 0:
+                lab_hop(d, step).wait_send()
 
     def finish(xs, _):
         for d in (0, 1):
@@ -434,17 +466,44 @@
     lax.fori_loop(0, NX, finish, 0)
 
 
+def finish_kernel(done, res, h_v, hess_l, out_ref, ob, sem):
+    z = lax.axis_index("dp")
+    o = lax.rem(z + 4, NZ)
+
+    def rows_at(k):
+        return pl.ds(pl.multiple_of(k * OWN, OWN), OWN)
+
+    copies = []
+    for k in range(1, NZ):
+        rws = rows_at(lax.rem(o + k, NZ))
+        copies.append(pltpu.make_async_copy(done.at[rws], out_ref.at[rws], sem.at[k]))
+        copies[-1].start()
+    for n in range(WIDTH // 256):
+        cols = slice(256 * n, 256 * (n + 1))
+        sums = jnp.dot(res[...], h_v[:, cols], preferred_element_type=F32)
+        ob[:, cols] = step_of(sums, hess_l[:, cols])
+        copies.append(pltpu.make_async_copy(ob.at[:, cols], out_ref.at[rows_at(o), cols], sem.at[NZ + n]))
+        copies[-1].start()
+    for c in copies:
+        c.wait()
+
+
 def local(hidden, labels, head_weight, hess_old):
     dma = pltpu.SemaphoreType.DMA
-    return pl.pallas_call(
+    vmem = pl.BlockSpec(memory_space=pltpu.VMEM)
+    parts = pl.pallas_call(
         kernel,
-        out_shape=pltpu.VMEM(hess_old.shape, BF16),
-        in_specs=[pl.BlockSpec(memory_space=pl.ANY)] * 4,
-        out_specs=pl.BlockSpec(memory_space=pltpu.VMEM),
+        out_shape=(
+            pltpu.VMEM(hess_old.shape, BF16),
+            pltpu.VMEM((OWN, TOK), BF16),
+            pltpu.VMEM((TOK, WIDTH), BF16),
+            pltpu.VMEM((OWN, WIDTH), BF16),
+        ),
+        in_specs=[pl.BlockSpec(memory_space=pltpu.HBM)] * 4,
+        out_specs=(vmem,) * 4,
         scratch_shapes=[
             pltpu.VMEM((NZ * OWN, WIDTH), BF16),
             pltpu.VMEM((NZ * OWN, WIDTH), BF16),
-            pltpu.VMEM((TOK, WIDTH), BF16),
             pltpu.VMEM((NZ, 1, 128), jnp.int32),
             pltpu.VMEM((16, 128), jnp.int32),
             pltpu.VMEM((8, 128), jnp.int32),
@@ -462,10 +521,9 @@
             pltpu.VMEM((NX, 16, 128), F32),
             pltpu.VMEM((NZ, 24, 128), F32),
             pltpu.VMEM((16, 128), F32),
-            pltpu.VMEM((OWN, TOK), BF16),
-            dma((4,)),
+            dma((5,)),
             dma((16,)), dma((16,)), dma((16,)), dma((16,)),
-            dma((7,)), dma((7,)),
+            dma((2, 4)), dma((2, 4)),
             dma((2, NX, 4)), dma((2, NX, 4)),
             dma((2, NX, 4)), dma((2, NX, 4)),
             dma((2, NX, 4)), dma((2, NX, 4)),
@@ -481,6 +539,16 @@
             flops=8 * TOK * NZ * OWN * WIDTH, bytes_accessed=13 * 2**20, transcendentals=TOK * NZ * OWN
         ),
     )(hidden, labels.reshape(1, 128), head_weight, hess_old)
+    parts = [pltpu.with_memory_space_constraint(p, pltpu.VMEM) for p in parts]
+    return pl.pallas_call(
+        finish_kernel,
+        out_shape=jax.ShapeDtypeStruct(hess_old.shape, BF16),
+        in_specs=[vmem] * 4,
+        out_specs=pl.BlockSpec(memory_space=pl.ANY),
+        scratch_shapes=[pltpu.VMEM((OWN, WIDTH), BF16), dma((NZ + WIDTH // 256,))],
+        compiler_params=pltpu.CompilerParams(vmem_limit_bytes=16 * 2**20),
+        cost_estimate=pl.CostEstimate(flops=2 * TOK * OWN * WIDTH, bytes_accessed=5 * 2**20, transcendentals=0),
+    )(*parts)
 
 
 def solution(mesh):

time: 109 us -> 105 us (0.963)
  local copies, waits for them, and re-layouts: 2.02 us -> 0 us
  Pallas kernels: 107 us -> 105 us
    unnamed x1 -> x0, local copies, waits for them, and re-layouts: 2.02 us -> none
    pallas_call x1 -> x2, Pallas kernels: 107 us -> 105 us  [the longest x1 103 us: local(): pl.pallas_call(kernel, out_shape=(pltpu.VMEM(hess_old.shape, BF16), pltpu...]
where the time goes in v3:
time: 105 us
  Pallas kernels  105 us (100%)
    pallas_call x1, Pallas kernels, local(): pl.pallas_call(kernel, out_shape=(pltpu.VMEM(hess_old.shape, BF16), pltpu...  103 us
    pallas_call x1, Pallas kernels, local(): pl.pallas_call(finish_kernel, out_shape=jax.ShapeDtypeStruct(hess_old.sha...  2.11 us

profile of v3, /device:TPU:1, one launch (start us, length us, event | category | flops | bytes accessed | tf_op | source)
XLA Modules:
  0.0 105.2 jit_solution(13127086068862510515)
XLA Ops:
  0.0 103.1 %shard_map.46 = (bf16[2048,1024]{1,0:T(8,128)(2,1)S(1)}, bf16[256,1024]{1,0:T(8,128)(2,1)S(1)}, bf16[1024,1024]{1,0:T(8,128)(2,1)S(1)}, bf16[256,1024]{1,0:T(8,128)(2,1)S(1)}) custom-call(bf16[32,1024]{1,0:T(8,128)(2,1)} %hid_ref.1, s32[1,128]{1,0:T(1,128)} %bitcast.1, bf16[2048,1024]{1,0:T(8,128)(2,1)} %w_ref.1, bf16[2048,1024]{1,0:T(8,128)(2,1)} %hess_ref.1), custom_call_target="tpu_custom_call" | custom-call | flops 17179869184 | bytes 13631488 | tf_op jit(solution)/shard_map/pallas_call | solution.py:494
  103.1 2.1 %shard_map.47 = bf16[2048,1024]{1,0:T(8,128)(2,1)} custom-call(bf16[2048,1024]{1,0:T(8,128)(2,1)S(1)} %get-tuple-element.9.done, bf16[256,1024]{1,0:T(8,128)(2,1)S(1)} %get-tuple-element.10.res, bf16[1024,1024]{1,0:T(8,128)(2,1)S(1)} %get-tuple-element.11.h_v, bf16[256,1024]{1,0:T(8,128)(2,1)S(1)} %get-tuple-element.12.hess_l), custom_call_target="tpu_custom_call" | custom-call | flops 536870912 | bytes 5242880 | tf_op jit(solution)/shard_map/pallas_call | solution.py:543

commit v4 on v3

--- a/solution.py
+++ b/solution.py
@@ -49,15 +49,15 @@
 
 
 def step_of(sums, old):
-    fresh = 0.9 * old.astype(F32) + 0.1 * sums * sums
-    return jnp.clip(sums / (10000.0 * fresh), -1.0, 1.0).astype(BF16)
+    scaled = 9000.0 * old.astype(F32) + 1000.0 * sums * sums
+    return jnp.clip(sums / scaled, -1.0, 1.0).astype(BF16)
 
 
 def kernel(
     hid_ref, lab_ref, w_ref, hess_ref, out_ref, res, h_v, hess_l,
-    w_v, hess_v, lab_v, lab_t, lab_l, part, mb, rb, rf, bb, lg, st_l, st, st_f, st_sib, st_y, st_x, st_z, stat,
+    w_v, hess_v, lab_v, lab_t, lab_l, part, mb, rb, rf, bb, lg, st_l, st, st_f, st_sib, st_y, st_q, st_x, st_z, bd, stat,
     loc_sem, g_send, g_recv, f_send, f_recv, lab_send, lab_recv, rs_send, rs_recv, bs_send, bs_recv,
-    ag_send, ag_recv, sy_send, sy_recv, sx_send, sx_recv, sib_send, sib_recv, sz_send, sz_recv,
+    ag_send, ag_recv, sy_send, sy_recv, sx_send, sx_recv, sf_send, sf_recv, bd_send, bd_recv, sib_send, sib_recv, sz_send, sz_recv,
 ):
     z = lax.axis_index("dp")
     v = lax.axis_index("vocab")
@@ -91,7 +91,6 @@
     far = pl.ds(pl.multiple_of(zmod(z + 4) * OWN, OWN), OWN)
     far_copy = pltpu.make_async_copy(hess_ref.at[far], hess_l, loc_sem.at[4])
     own_copy = pltpu.make_async_copy(hid_ref, slot(0, core), loc_sem.at[3])
-    w_copy.start()
     lab_copy.start()
     own_copy.start()
 
@@ -108,16 +107,18 @@
     pl.semaphore_wait(barrier, len(partners))
 
     def hop(k, c, step):
-        src = hid_ref if k == 0 else slot(k, core)
+        src = slot(k, core)
         return remote(src, slot(c, core), g_send.at[c], g_recv.at[c], at(*step))
 
     def share(k):
         src = hid_ref if k == 0 else slot(k, core)
         return remote(src, slot(k, core), f_send.at[k], f_recv.at[k], sib)
 
+    own_copy.wait()
     for c, step in HOPS[0][:4]:
         hop(0, c, step).start()
     share(0).start()
+    w_copy.start()
     def lab_hop(d, step):
         o = zmod(z + 1 - step) if d == 0 else zmod(z - 1 + step)
         return remote(lab_v.at[o], lab_v.at[o], lab_send.at[d, step - 1], lab_recv.at[d, step - 1], zring[d])
@@ -125,7 +126,6 @@
     lab_copy.wait()
     for d in (0, 1):
         lab_hop(d, 1).start()
-    own_copy.wait()
     w_copy.wait()
     for c, step in HOPS[0][:4]:
         hop(0, c, step).wait_send()
@@ -155,20 +155,29 @@
     def to_int(q):
         return jnp.round(q).astype(I16)
 
-    def first(d, xs, place, o, half):
-        b = mb[xs, o, half : half + 1, :]
+    def first(d, xs, far_o, next_o):
+        b = jnp.maximum(mb[xs, far_o, d : d + 1, :], mb[xs, next_o, 1 - d : 2 - d, :])
         scale = TOP / jnp.maximum(b, TINY)
-        rb[d, xs, 0, place * HALF : (place + 1) * HALF, :] = to_int(rows_of(xs, o, half) * scale)
-        bb[d, xs, 0, place : place + 1, :] = b
-
-    def fold(d, xs, slot, place, o, half):
-        b_in = bb[d, xs, slot, place : place + 1, :]
-        b = b_in + mb[xs, o, half : half + 1, :]
+        rb[d, xs, 0, :HALF, :] = to_int(rows_of(xs, far_o, d) * scale)
+        rb[d, xs, 0, HALF:, :] = to_int(rows_of(xs, next_o, 1 - d) * scale)
+        bb[d, xs, 0] = b
+
+    def fold(d, xs, slot, far_o, next_o):
+        b_in = bb[d, xs, slot]
+        b = mb[xs, far_o, d : d + 1, :]
+        if next_o is not None:
+            b = jnp.maximum(b, mb[xs, next_o, 1 - d : 2 - d, :])
+        b = b_in + b
         inv = 1.0 / jnp.maximum(b, TINY)
-        got = rb[d, xs, slot, place * HALF : (place + 1) * HALF, :].astype(F32)
-        q = got * (b_in * inv) + rows_of(xs, o, half) * (TOP * inv)
-        rb[d, xs, slot, place * HALF : (place + 1) * HALF, :] = to_int(q)
-        bb[d, xs, slot, place : place + 1, :] = b
+        old, new = b_in * inv, TOP * inv
+        upper = rb[d, xs, slot, :HALF, :].astype(F32)
+        rb[d, xs, slot, :HALF, :] = to_int(upper * old + rows_of(xs, far_o, d) * new)
+        if next_o is None:
+            bb[d, xs, 5] = b
+            return
+        lower = rb[d, xs, slot, HALF:, :].astype(F32)
+        rb[d, xs, slot, HALF:, :] = to_int(lower * old + rows_of(xs, next_o, 1 - d) * new)
+        bb[d, xs, slot] = b
 
     def rs_data(d, xs, s):
         if not isinstance(s, int) or s < 4:
@@ -178,9 +187,8 @@
         return remote(src, dst, rs_send.at[d, xs, s - 1], rs_recv.at[d, xs, s - 1], zring[d])
 
     def rs_bound(d, xs, s):
-        return remote(
-            bb.at[d, xs, s - 1], bb.at[d, xs, s], bs_send.at[d, xs, s - 1], bs_recv.at[d, xs, s - 1], zring[d]
-        )
+        src = bb.at[d, xs, 5] if isinstance(s, int) and s == 4 else bb.at[d, xs, s - 1]
+        return remote(src, bb.at[d, xs, s], bs_send.at[d, xs, s - 1], bs_recv.at[d, xs, s - 1], zring[d])
 
     def rs_start(d, xs, s):
         rs_bound(d, xs, s).start()
@@ -207,12 +215,10 @@
                 return 0
 
             lax.fori_loop(0, 2, owners, 0)
-            first(0, i, 0, zmod(z + 4), 0)
-            first(0, i, 1, zmod(z + 3), 1)
+            first(0, i, zmod(z + 4), zmod(z + 3))
             rs_start(0, i, 1)
             lax.fori_loop(2, 3, owners, 0)
-            first(1, i, 0, zmod(z - 4), 1)
-            first(1, i, 1, zmod(z - 3), 0)
+            first(1, i, zmod(z - 4), zmod(z - 3))
             rs_start(1, i, 1)
 
         @pl.when(s > 1)
@@ -223,12 +229,10 @@
 
             lax.fori_loop(0, 2, owners, 0)
             rs_wait(0, i, s - 1)
-            fold(0, i, s - 1, 0, zmod(z + 5 - s), 0)
-            fold(0, i, s - 1, 1, zmod(z + 4 - s), 1)
+            fold(0, i, s - 1, zmod(z + 5 - s), zmod(z + 4 - s))
             rs_start(0, i, s)
             rs_wait(1, i, s - 1)
-            fold(1, i, s - 1, 0, zmod(z - 5 + s), 1)
-            fold(1, i, s - 1, 1, zmod(z - 4 + s), 0)
+            fold(1, i, s - 1, zmod(z - 5 + s), zmod(z - 4 + s))
             rs_start(1, i, s)
 
         for step in (1, 2, 3):
@@ -250,10 +254,10 @@
     def step4(i, _):
         xs = i
         rs_wait(0, xs, 3)
-        fold(0, xs, 3, 0, zmod(z + 1), 0)
+        fold(0, xs, 3, zmod(z + 1), None)
         rs_start(0, xs, 4)
         rs_wait(1, xs, 3)
-        fold(1, xs, 3, 0, zmod(z - 1), 1)
+        fold(1, xs, 3, zmod(z - 1), None)
         rs_start(1, xs, 4)
         mm(xs, z)
         return 0
@@ -278,8 +282,8 @@
         xs = i
         rs_wait(0, xs, 4)
         rs_wait(1, xs, 4)
-        b0, b1 = bb[0, xs, 4, 0:1, :], bb[1, xs, 3, 1:2, :]
-        c0, c1 = bb[1, xs, 4, 0:1, :], bb[0, xs, 3, 1:2, :]
+        b0, b1 = bb[0, xs, 4], bb[1, xs, 3]
+        c0, c1 = bb[1, xs, 4], bb[0, xs, 3]
         k = 1.0 / TOP
         upper = rows_of(xs, z, 0) + rf[0, xs].astype(F32) * (b0 * k) + rb[1, xs, 3, HALF:, :].astype(F32) * (b1 * k)
         lower = rows_of(xs, z, 1) + rf[1, xs].astype(F32) * (c0 * k) + rb[0, xs, 3, HALF:, :].astype(F32) * (c1 * k)
@@ -296,13 +300,12 @@
             lanes = slice(128 * j, 128 * (j + 1))
             st_l[pl.ds(2 * xs + j, 1), :] = m[:, lanes]
             st_l[pl.ds(8 + 2 * xs + j, 1), :] = e[:, lanes]
-            st_z[z, pl.ds(16 + 2 * xs + j, 1), :] = b[:, lanes] * k
+            bd[z, pl.ds(2 * xs + j, 1), :] = b[:, lanes] * k
         return 0
 
     lax.fori_loop(0, NX, total, 0)
 
     left8 = lax.broadcasted_iota(jnp.int32, (8, 128), 1) < 64
-    left16 = lax.broadcasted_iota(jnp.int32, (16, 128), 1) < 64
 
     def swap(a):
         return pltpu.roll(a, 64, 1)
@@ -314,7 +317,7 @@
         e = jnp.zeros_like(m)
         for a in parts:
             e = e + a * swap(jnp.exp(a - m))
-        return jnp.where(left16, m, e)
+        return jnp.where(lax.broadcasted_iota(jnp.int32, m.shape, 1) < 64, m, e)
 
     m, e = st_l[0:8], st_l[8:16]
     even, odd = jnp.where(left8, m, swap(e)), jnp.where(left8, swap(m), e)
@@ -324,12 +327,16 @@
 
     sib_copy = remote(st, st_sib, sib_send, sib_recv, sib)
     ycopies = [remote(st_y.at[0], st_y.at[d], sy_send.at[d], sy_recv.at[d], ypeers[d - 1]) for d in range(1, NY)]
-    xcopies = [remote(st_x.at[0], st_x.at[d], sx_send.at[d], sx_recv.at[d], xpeers[d - 1]) for d in range(1, NX)]
+    xcopies = [
+        remote(st_q.at[lax.rem(x + d, NX)], st_x.at[d], sx_send.at[d], sx_recv.at[d], xpeers[d - 1]) for d in range(1, NX)
+    ]
     zcopies = [remote(st_z.at[z], st_z.at[z], sz_send.at[k], sz_recv.at[k], dev) for k, dev in enumerate(zpeers)]
+    bcopies = [remote(bd.at[z], bd.at[z], bd_send.at[k], bd_recv.at[k], dev) for k, dev in enumerate(zpeers)]
+    fcopies = [remote(st_f.at[x], st_f.at[x], sf_send.at[d], sf_recv.at[d], xpeers[d - 1]) for d in range(1, NX)]
     sib_copy.start()
     sib_copy.wait_recv()
     st_y[0] = merge([st[...], st_sib[...]])
-    for g in ycopies:
+    for g in ycopies + bcopies:
         g.start()
 
     def ag_next(i, s):
@@ -344,15 +351,18 @@
         def _():
             for g in ycopies:
                 g.wait_recv()
-            st_x[0] = merge([st_y[d] for d in range(NY)])
+            m = merge([st_y[d] for d in range(NY)])
+            for c in range(NX):
+                st_q[c] = m[NY * c : NY * (c + 1)]
+            st_x[0] = st_q[x]
             for g in xcopies:
                 g.start()
 
-        @pl.when(i == 3)
+        @pl.when(i == 2)
         def _():
             for g in xcopies:
                 g.wait_recv()
-            st_z[z, 0:16] = merge([st_x[d] for d in range(NX)])
+            st_z[z] = merge([st_x[d] for d in range(NX)])
             for g in zcopies:
                 g.start()
 
@@ -360,21 +370,31 @@
 
     lax.fori_loop(0, NX, ag_two, 0)
 
-    def settle():
+    def cross():
         for k in range(NZ - 1):
             o = zmod(z - 1 - k)
             remote(st_z.at[o], st_z.at[o], sz_send.at[k], sz_recv.at[k], sib).wait_recv()
+        st_f[x] = merge([st_z[o] for o in range(NZ)])
+        for g in fcopies:
+            g.start()
+
+    def settle():
+        for d in range(1, NX):
+            c = lax.rem(x + NX - d, NX)
+            remote(st_f.at[c], st_f.at[c], sf_send.at[d], sf_recv.at[d], sib).wait_recv()
+        for k in range(NZ - 1):
+            o = zmod(z - 1 - k)
+            remote(bd.at[o], bd.at[o], bd_send.at[k], bd_recv.at[k], sib).wait_recv()
         lab_hop(0, 4).wait_recv()
         hess_copy.wait()
         far_copy.wait()
-        st_f[...] = merge([st_z[o, 0:16] for o in range(NZ)])
         for r in range(8):
             lab_t[r : r + 1, :] = lab_v[r]
         lab_t[8:16] = swap(lab_t[0:8])
         for r in range(8):
             a, b = chip_of(2 * r), chip_of(2 * r + 1)
-            st_l[r : r + 1, :] = st_f[pl.ds(a, 1), :]
-            st_l[8 + r : 9 + r, :] = st_f[pl.ds(b, 1), :]
+            st_l[r : r + 1, :] = st_f[a // NY, pl.ds(lax.rem(a, NY), 1), :]
+            st_l[8 + r : 9 + r, :] = st_f[b // NY, pl.ds(lax.rem(b, NY), 1), :]
             lab_l[r : r + 1, :] = jnp.where(
                 left8[0:1], lab_t[pl.ds(a // 2 + 8 * lax.rem(a, 2), 1), :], lab_t[pl.ds(b // 2 + 8 * (1 - lax.rem(b, 2)), 1), :]
             )
@@ -387,7 +407,7 @@
         for h in range(2):
             r = 2 * i + h
             top, inv = stat[pl.ds(r, 1), :], stat[pl.ds(8 + r, 1), :]
-            scale = st_z[o, pl.ds(16 + r, 1), :]
+            scale = bd[o, pl.ds(r, 1), :]
             lab = lab_l[pl.ds(r, 1), :]
             for q in range(4):
                 sub = slice(64 * q, 64 * (q + 1))
@@ -410,6 +430,10 @@
 
         @pl.when(k == 0)
         def _():
+            cross()
+
+        @pl.when(k == 1)
+        def _():
             settle()
 
         @pl.when((k >= NX) & (k < 2 * NX))
@@ -448,7 +472,7 @@
         remote(slot(c, core), slot(c, core), g_send.at[c], g_recv.at[c], sib).wait_send()
     for k in range(16):
         share(k).wait_send()
-    for g in [sib_copy] + ycopies + xcopies + zcopies:
+    for g in [sib_copy] + ycopies + xcopies + zcopies + bcopies + fcopies:
         g.wait_send()
     for step in (1, 2, 3, 4):
         for d in (0, 1):
@@ -511,15 +535,17 @@
             pltpu.VMEM((NX, NZ, 2, SB), F32),
             pltpu.VMEM((2, NX, 4, OWN, SB), I16),
             pltpu.VMEM((2, NX, HALF, SB), I16),
-            pltpu.VMEM((2, NX, 5, 2, SB), F32),
+            pltpu.VMEM((2, NX, 6, 1, SB), F32),
             pltpu.VMEM((NZ, NX, OWN, SB), I16),
             pltpu.VMEM((16, 128), F32),
             pltpu.VMEM((16, 128), F32),
-            pltpu.VMEM((16, 128), F32),
+            pltpu.VMEM((NX, NY, 128), F32),
             pltpu.VMEM((16, 128), F32),
             pltpu.VMEM((NY, 16, 128), F32),
-            pltpu.VMEM((NX, 16, 128), F32),
-            pltpu.VMEM((NZ, 24, 128), F32),
+            pltpu.VMEM((NX, NY, 128), F32),
+            pltpu.VMEM((NX, NY, 128), F32),
+            pltpu.VMEM((NZ, NY, 128), F32),
+            pltpu.VMEM((NZ, 8, 128), F32),
             pltpu.VMEM((16, 128), F32),
             dma((5,)),
             dma((16,)), dma((16,)), dma((16,)), dma((16,)),
@@ -529,6 +555,8 @@
             dma((2, NX, 4)), dma((2, NX, 4)),
             dma((NY,)), dma((NY,)),
             dma((NX,)), dma((NX,)),
+            dma((NX,)), dma((NX,)),
+            dma((7,)), dma((7,)),
             dma, dma,
             dma((7,)), dma((7,)),
         ],

time: 105 us -> 103 us (0.981)
  Pallas kernels: 105 us -> 103 us
    pallas_call x1, Pallas kernels: 103 us -> 101 us  [local(): pl.pallas_call(kernel, out_shape=(pltpu.VMEM(hess_old.shape, BF16), pltpu...]
where the time goes in v4:
time: 103 us
  Pallas kernels  103 us (100%)
    pallas_call x1, Pallas kernels, local(): pl.pallas_call(kernel, out_shape=(pltpu.VMEM(hess_old.shape, BF16), pltpu...  101 us
    pallas_call x1, Pallas kernels, local(): pl.pallas_call(finish_kernel, out_shape=jax.ShapeDtypeStruct(hess_old.sha...  2.11 us

profile of v4, /device:TPU:1, one launch (start us, length us, event | category | flops | bytes accessed | tf_op | source)
XLA Modules:
  0.0 102.9 jit_solution(809100261155542483)
XLA Ops:
  0.0 100.8 %shard_map.46 = (bf16[2048,1024]{1,0:T(8,128)(2,1)S(1)}, bf16[256,1024]{1,0:T(8,128)(2,1)S(1)}, bf16[1024,1024]{1,0:T(8,128)(2,1)S(1)}, bf16[256,1024]{1,0:T(8,128)(2,1)S(1)}) custom-call(bf16[32,1024]{1,0:T(8,128)(2,1)} %hid_ref.1, s32[1,128]{1,0:T(1,128)} %bitcast.1, bf16[2048,1024]{1,0:T(8,128)(2,1)} %w_ref.1, bf16[2048,1024]{1,0:T(8,128)(2,1)} %hess_ref.1), custom_call_target="tpu_custom_call" | custom-call | flops 17179869184 | bytes 13631488 | tf_op jit(solution)/shard_map/pallas_call | solution.py:518
  100.8 2.1 %shard_map.47 = bf16[2048,1024]{1,0:T(8,128)(2,1)} custom-call(bf16[2048,1024]{1,0:T(8,128)(2,1)S(1)} %get-tuple-element.9.done, bf16[256,1024]{1,0:T(8,128)(2,1)S(1)} %get-tuple-element.10.res, bf16[1024,1024]{1,0:T(8,128)(2,1)S(1)} %get-tuple-element.11.h_v, bf16[256,1024]{1,0:T(8,128)(2,1)S(1)} %get-tuple-element.12.hess_l), custom_call_target="tpu_custom_call" | custom-call | flops 536870912 | bytes 5242880 | tf_op jit(solution)/shard_map/pallas_call | solution.py:571

commit v5 on v4

--- a/solution.py
+++ b/solution.py
@@ -55,7 +55,7 @@
 
 def kernel(
     hid_ref, lab_ref, w_ref, hess_ref, out_ref, res, h_v, hess_l,
-    w_v, hess_v, lab_v, lab_t, lab_l, part, mb, rb, rf, bb, lg, st_l, st, st_f, st_sib, st_y, st_q, st_x, st_z, bd, stat,
+    w_v, hess_v, lab_v, lab_t, lab_l, part, rb, rf, bb, lg, st_l, st, st_f, st_sib, st_y, st_q, st_x, st_z, bd, stat,
     loc_sem, g_send, g_recv, f_send, f_recv, lab_send, lab_recv, rs_send, rs_recv, bs_send, bs_recv,
     ag_send, ag_recv, sy_send, sy_recv, sx_send, sx_recv, sf_send, sf_recv, bd_send, bd_recv, sib_send, sib_recv, sz_send, sz_recv,
 ):
@@ -146,38 +146,36 @@
         b = h_v[pl.ds(pl.multiple_of(xs * SB, SB), SB), :]
         p = lax.dot_general(a, b, (((1,), (1,)), ((), ())), preferred_element_type=F32)
         part[xs, o] = p
-        mb[xs, o, 0:1, :] = jnp.max(jnp.abs(p[:HALF]), axis=0, keepdims=True)
-        mb[xs, o, 1:2, :] = jnp.max(jnp.abs(p[HALF:]), axis=0, keepdims=True)
 
     def rows_of(xs, o, half):
         return part[xs, o, half * HALF : (half + 1) * HALF, :]
 
+    def largest(a):
+        return jnp.maximum(jnp.max(jnp.abs(a), axis=0, keepdims=True), TINY)
+
     def to_int(q):
         return jnp.round(q).astype(I16)
 
     def first(d, xs, far_o, next_o):
-        b = jnp.maximum(mb[xs, far_o, d : d + 1, :], mb[xs, next_o, 1 - d : 2 - d, :])
-        scale = TOP / jnp.maximum(b, TINY)
-        rb[d, xs, 0, :HALF, :] = to_int(rows_of(xs, far_o, d) * scale)
-        rb[d, xs, 0, HALF:, :] = to_int(rows_of(xs, next_o, 1 - d) * scale)
-        bb[d, xs, 0] = b
+        upper, lower = rows_of(xs, far_o, d), rows_of(xs, next_o, 1 - d)
+        b = jnp.maximum(largest(upper), largest(lower))
+        rb[d, xs, 0, :HALF, :] = to_int(upper * (TOP / b))
+        rb[d, xs, 0, HALF:, :] = to_int(lower * (TOP / b))
+        bb[d, xs, 0] = b * (1.0 / TOP)
 
     def fold(d, xs, slot, far_o, next_o):
         b_in = bb[d, xs, slot]
-        b = mb[xs, far_o, d : d + 1, :]
-        if next_o is not None:
-            b = jnp.maximum(b, mb[xs, next_o, 1 - d : 2 - d, :])
-        b = b_in + b
-        inv = 1.0 / jnp.maximum(b, TINY)
-        old, new = b_in * inv, TOP * inv
-        upper = rb[d, xs, slot, :HALF, :].astype(F32)
-        rb[d, xs, slot, :HALF, :] = to_int(upper * old + rows_of(xs, far_o, d) * new)
+        upper = rb[d, xs, slot, :HALF, :].astype(F32) * b_in + rows_of(xs, far_o, d)
+        b = largest(upper)
         if next_o is None:
-            bb[d, xs, 5] = b
+            rb[d, xs, slot, :HALF, :] = to_int(upper * (TOP / b))
+            bb[d, xs, 5] = b * (1.0 / TOP)
             return
-        lower = rb[d, xs, slot, HALF:, :].astype(F32)
-        rb[d, xs, slot, HALF:, :] = to_int(lower * old + rows_of(xs, next_o, 1 - d) * new)
-        bb[d, xs, slot] = b
+        lower = rb[d, xs, slot, HALF:, :].astype(F32) * b_in + rows_of(xs, next_o, 1 - d)
+        b = jnp.maximum(b, largest(lower))
+        rb[d, xs, slot, :HALF, :] = to_int(upper * (TOP / b))
+        rb[d, xs, slot, HALF:, :] = to_int(lower * (TOP / b))
+        bb[d, xs, slot] = b * (1.0 / TOP)
 
     def rs_data(d, xs, s):
         if not isinstance(s, int) or s < 4:
@@ -284,11 +282,9 @@
         rs_wait(1, xs, 4)
         b0, b1 = bb[0, xs, 4], bb[1, xs, 3]
         c0, c1 = bb[1, xs, 4], bb[0, xs, 3]
-        k = 1.0 / TOP
-        upper = rows_of(xs, z, 0) + rf[0, xs].astype(F32) * (b0 * k) + rb[1, xs, 3, HALF:, :].astype(F32) * (b1 * k)
-        lower = rows_of(xs, z, 1) + rf[1, xs].astype(F32) * (c0 * k) + rb[0, xs, 3, HALF:, :].astype(F32) * (c1 * k)
-        b = jnp.maximum(mb[xs, z, 0:1, :] + b0 + b1, mb[xs, z, 1:2, :] + c0 + c1)
-        b = jnp.maximum(b, TINY)
+        upper = rows_of(xs, z, 0) + rf[0, xs].astype(F32) * b0 + rb[1, xs, 3, HALF:, :].astype(F32) * b1
+        lower = rows_of(xs, z, 1) + rf[1, xs].astype(F32) * c0 + rb[0, xs, 3, HALF:, :].astype(F32) * c1
+        b = jnp.maximum(largest(upper), largest(lower))
         scale = TOP / b
         lg[z, xs, :HALF, :] = to_int(upper * scale)
         lg[z, xs, HALF:, :] = to_int(lower * scale)
@@ -300,7 +296,7 @@
             lanes = slice(128 * j, 128 * (j + 1))
             st_l[pl.ds(2 * xs + j, 1), :] = m[:, lanes]
             st_l[pl.ds(8 + 2 * xs + j, 1), :] = e[:, lanes]
-            bd[z, pl.ds(2 * xs + j, 1), :] = b[:, lanes] * k
+            bd[z, pl.ds(2 * xs + j, 1), :] = b[:, lanes] * (1.0 / TOP)
         return 0
 
     lax.fori_loop(0, NX, total, 0)
@@ -532,7 +528,6 @@
             pltpu.VMEM((16, 128), jnp.int32),
             pltpu.VMEM((8, 128), jnp.int32),
             pltpu.VMEM((NX, NZ, OWN, SB), F32),
-            pltpu.VMEM((NX, NZ, 2, SB), F32),
             pltpu.VMEM((2, NX, 4, OWN, SB), I16),
             pltpu.VMEM((2, NX, HALF, SB), I16),
             pltpu.VMEM((2, NX, 6, 1, SB), F32),

time: 103 us -> 103 us (level)
  no operation moved by 1% of the time
where the time goes in v5:
time: 103 us
  Pallas kernels  103 us (100%)
    pallas_call x1, Pallas kernels, local(): pl.pallas_call(kernel, out_shape=(pltpu.VMEM(hess_old.shape, BF16), pltpu...  101 us
    pallas_call x1, Pallas kernels, local(): pl.pallas_call(finish_kernel, out_shape=jax.ShapeDtypeStruct(hess_old.sha...  2.11 us

profile of v5, /device:TPU:1, one launch (start us, length us, event | category | flops | bytes accessed | tf_op | source)
XLA Modules:
  0.0 102.9 jit_solution(15165585723616865542)
XLA Ops:
  0.0 100.8 %shard_map.46 = (bf16[2048,1024]{1,0:T(8,128)(2,1)S(1)}, bf16[256,1024]{1,0:T(8,128)(2,1)S(1)}, bf16[1024,1024]{1,0:T(8,128)(2,1)S(1)}, bf16[256,1024]{1,0:T(8,128)(2,1)S(1)}) custom-call(bf16[32,1024]{1,0:T(8,128)(2,1)} %hid_ref.1, s32[1,128]{1,0:T(1,128)} %bitcast.1, bf16[2048,1024]{1,0:T(8,128)(2,1)} %w_ref.1, bf16[2048,1024]{1,0:T(8,128)(2,1)} %hess_ref.1), custom_call_target="tpu_custom_call" | custom-call | flops 17179869184 | bytes 13631488 | tf_op jit(solution)/shard_map/pallas_call | solution.py:514
  100.8 2.1 %shard_map.47 = bf16[2048,1024]{1,0:T(8,128)(2,1)} custom-call(bf16[2048,1024]{1,0:T(8,128)(2,1)S(1)} %get-tuple-element.9.done, bf16[256,1024]{1,0:T(8,128)(2,1)S(1)} %get-tuple-element.10.res, bf16[1024,1024]{1,0:T(8,128)(2,1)S(1)} %get-tuple-element.11.h_v, bf16[256,1024]{1,0:T(8,128)(2,1)S(1)} %get-tuple-element.12.hess_l), custom_call_target="tpu_custom_call" | custom-call | flops 536870912 | bytes 5242880 | tf_op jit(solution)/shard_map/pallas_call | solution.py:566
